TPU v7x, 32 devices: a whole 2x2x4 slice. The times are simulated.
32 devices in a mesh: patch: 2 (over x), epoch: 16 (over z, y, core).
Axes of the slice: x: 2, y: 2, z: 4, core: 2. Of those that a mesh axis runs over, the one named last changes fastest.
Arguments:
- epoch_images: float32 [32, 64, 4096], P(('patch', 'epoch')), parts along dimension 0, may hold values from -8 to 8
- mask_words: int32 [32, 1, 128], P(('patch', 'epoch')), parts along dimension 0, may hold values from -2147483648 to 2147483647, as said below
- coefficients: float32 [32, 49, 3], P('patch'), parts along dimension 0, may hold values from -2 to 2
- epoch_order: int32 [32], P('patch'), parts along dimension 0, may hold values from 0 to 15, each once
Outputs:
- difference: float32 [32, 32, 4096], P(('patch', 'epoch')), parts along dimension 0
There are 2 independent parts, one for each index of `patch`. A program takes and returns all parts, laid end to end along the dimension named above; each array names one. Nothing has to cross between parts.
Inputs may be any that keep to these rules, and one draw needn't show every extreme that they name: `mask_words`: bit b of word w in band n of an epoch marks column 32 w + b of rows n * 64 to (n + 1) * 64 - 1 of that epoch valid (1) or masked (0), bit 31 being the sign bit; some cells are masked in every epoch. A permutation: image slot e uses the coefficients of catalog epoch epoch_order[e].
All inputs are finite; a program needn't handle non-finite values.
Results may differ from a plain program's by a relative error of at most 0.000057.
Values sent between devices are 32-bit elements; how exact they have to be, the bound alone decides.
A program may use at most 64 MiB of HBM per device.

v0:
```python
import math

import jax
import jax.numpy as jnp
import numpy as np
from jax import lax
from jax.sharding import PartitionSpec as P

HALF = 15
MARGIN = 16
BAND = 64


gauss_widths = (1.5, 3.0, 6.0)
gauss_degrees = (6, 4, 2)


def extended(cells, sides, width):
    for axis, dim in sides:
        count = lax.axis_size(axis)
        ends = count - 1
        head = lax.slice_in_dim(cells, 0, width, axis=dim)
        tail = lax.slice_in_dim(cells, cells.shape[dim] - width, cells.shape[dim], axis=dim)
        cells = jnp.concatenate(
            [
                lax.ppermute(tail, axis, [(i, (i + 1) % count) for i in range(ends)]),
                cells,
                lax.ppermute(head, axis, [((i + 1) % count, i) for i in range(ends)]),
            ],
            axis=dim,
        )
    return cells


def basis_filters(half_width):
    offsets = jnp.arange(-half_width, half_width + 1).astype(jnp.float32)
    result = []
    for spread_width, degree in zip(gauss_widths, gauss_degrees):
        envelope = jnp.exp(-offsets * offsets / (2.0 * spread_width * spread_width)) / (
            math.sqrt(2.0 * math.pi) * spread_width
        )
        for vert_power in range(degree + 1):
            result.append(envelope * (offsets / spread_width) ** vert_power)
    return jnp.stack(result)


def kernel_pairs():
    result = []
    first_index = 0
    for degree in gauss_degrees:
        for vert_power in range(degree + 1):
            for horiz_power in range(degree + 1 - vert_power):
                result.append((first_index + vert_power, first_index + horiz_power))
        first_index = first_index + degree + 1
    return result


def unpack_valid(mask_words):
    bit_places = jnp.arange(32, dtype=jnp.int32)
    bit_values = jnp.right_shift(mask_words[..., None], bit_places) & 1
    word_shape = mask_words.shape
    return bit_values.reshape(word_shape[0], word_shape[1], word_shape[2] * 32).astype(jnp.float32)


def shift_table(tap_count, inner_cols, outer_cols):
    taps_axis = jnp.arange(tap_count)[:, None, None]
    inner_axis = jnp.arange(inner_cols)[None, :, None]
    outer_axis = jnp.arange(outer_cols)[None, None, :]
    return (inner_axis - outer_axis == taps_axis).astype(jnp.float32)


def vertical_matrices(filters, rows_out, padded_rows):
    tap_count = filters.shape[1]
    out_rows = jnp.arange(rows_out)[:, None]
    in_rows = jnp.arange(padded_rows)[None, :]
    places = in_rows - out_rows - MARGIN + HALF
    one_hot = (places[None] == jnp.arange(tap_count)[:, None, None]).astype(jnp.float32)
    return jnp.einsum("jd,drt->jrt", filters, one_hot, precision=lax.Precision.HIGHEST)


def spatial_terms(col_start, col_count, total_columns, rows_out):
    columns = (
        2.0 * (col_start + jnp.arange(col_count)).astype(jnp.float32) + 1.0
    ) / total_columns - 1.0
    row_pos = (2.0 * jnp.arange(rows_out).astype(jnp.float32) + 1.0) / rows_out - 1.0
    return jnp.stack(
        [
            jnp.ones((rows_out, col_count), jnp.float32),
            jnp.broadcast_to(columns[None, :], (rows_out, col_count)),
            jnp.broadcast_to(row_pos[:, None], (rows_out, col_count)),
        ]
    )


def shards(epoch_images, mask_words, coefficients, epoch_order):
    slot_count, padded_rows, total_columns = epoch_images.shape
    rows_out = padded_rows - 2 * MARGIN
    band_valid = unpack_valid(mask_words)
    valid_mask = jnp.repeat(band_valid, BAND, axis=1)
    part_total = jnp.sum(valid_mask * epoch_images, axis=0)
    part_count = jnp.sum(band_valid, axis=0)
    filters = basis_filters(HALF)
    pair_list = kernel_pairs()
    vert_table = np.zeros((len(pair_list), filters.shape[0]), np.float32)
    horiz_table = np.zeros((len(pair_list), filters.shape[0]), np.float32)
    for kernel_index, pair_value in enumerate(pair_list):
        vert_table[kernel_index, pair_value[0]] = 1.0
        horiz_table[kernel_index, pair_value[1]] = 1.0
    vert_pick = jnp.asarray(vert_table)
    horiz_filters = jnp.dot(jnp.asarray(horiz_table), filters, precision=lax.Precision.HIGHEST)
    vert_mats = vertical_matrices(filters, rows_out, padded_rows)
    full_sum, full_count = (
        lax.psum_scatter(part_total, "epoch", scatter_dimension=1, tiled=True),
        lax.psum_scatter(part_count, "epoch", scatter_dimension=1, tiled=True),
    )
    template = full_sum / jnp.maximum(jnp.repeat(full_count, BAND, axis=0), 1.0)
    slab_cols = template.shape[1]
    rimmed = extended(template, (("epoch", 1),), HALF)
    vertical = jnp.einsum("jrt,tc->jrc", vert_mats, rimmed, precision=lax.Precision.HIGHEST)
    picked = jnp.einsum("kj,jrc->krc", vert_pick, vertical, precision=lax.Precision.HIGHEST)
    horiz_mats = jnp.einsum(
        "kd,dso->kso",
        horiz_filters,
        shift_table(horiz_filters.shape[1], slab_cols + 2 * HALF, slab_cols),
        precision=lax.Precision.HIGHEST,
    )
    convolved = jnp.einsum("krs,kso->kro", picked, horiz_mats, precision=lax.Precision.HIGHEST)
    spatial = spatial_terms(lax.axis_index("epoch") * slab_cols, slab_cols, total_columns, rows_out)
    term_count = coefficients.shape[1] * coefficients.shape[2]
    basis_images = (convolved[:, None] * spatial[None]).reshape(term_count, rows_out * slab_cols)
    coef_table = coefficients[epoch_order].reshape(coefficients.shape[0], term_count)
    models = jnp.dot(
        coef_table,
        basis_images,
        precision=lax.Precision.HIGHEST,
        preferred_element_type=jnp.float32,
    ).reshape(coefficients.shape[0], rows_out, slab_cols)
    model_image = lax.all_to_all(models, "epoch", split_axis=0, concat_axis=2, tiled=True)
    centre = epoch_images[:, MARGIN : MARGIN + rows_out]
    return valid_mask[:, MARGIN : MARGIN + rows_out] * (centre - model_image)


def solution(mesh):
    placed = (
        P(("patch", "epoch"), None, None),
        P(("patch", "epoch"), None, None),
        P("patch", None, None),
        P("patch"),
    )
    return jax.shard_map(
        shards,
        mesh=mesh,
        in_specs=placed,
        out_specs=P(("patch", "epoch"), None, None),
        check_vma=False,
    )
```

profile of v0, /device:TPU:0, one launch (start us, length us, event | category | flops | bytes accessed | tf_op | source)
XLA Modules:
  0.0 205.3 jit_solution(17101479756316634492)
XLA Ops:
  6.8 0.8 shift_right_arithmetic.37
  7.6 0.1 shift_right_arithmetic.42
  7.7 0.1 shift_right_arithmetic.44
  7.9 2.0 copy.29
  9.9 0.1 shift_right_arithmetic.38
  10.0 0.1 shift_right_arithmetic.40
  10.1 1.1 multiply_bitcast_fusion
  11.5 0.1 stack.4
  11.6 0.1 stack_broadcast_in_dim.15
  11.7 0.1 pad_maximum_fusion
  11.8 0.3 fusion.9
  12.2 9.9 %fusion.2 = f32[49,286,256]{2,0,1:T(8,128)} fusion(s32[286,256]{1,0:T(8,128)S(1)} %iota_subtract_fusion, f32[49]{0:T(128)S(1)} %copy-done.3, f32[31]{0:T(128)S(1)} %fusion.70, f32[49]{0:T(128)S(1)} %copy-done.17, f32[31]{0:T(128)S(1)} %get-tuple-element.15, f32[49]{0:T(128)S(1)} %copy-done.16, f32[31]{0:T(128)S(1)} %get-tuple-element.9, ...), kind=kOutput, calls=%fused_computation.4 | convolution fusion | flops 1336894976 | bytes 14648000 | tf_op jit(solution)/shard_map/kd,dso->kso/dot_general | solution.py:121
  22.1 53.5 %reduce-scatter.7.cloned.1.call-done = f32[256,1]{1,0:T(8,128)} async-done(((f32[4096,1]{1,0:T(8,128)}), f32[256,1]{1,0:T(8,128)}) %reduce-scatter.7.cloned.1.call-update) | async-done | bytes 1040
  75.6 0.9 maximum_bitcast_fusion
  76.5 0.1 copy.34
  76.6 59.5 %reduce-scatter.5.cloned.1.call-done = f32[64,256]{1,0:T(8,128)} async-done(((f32[64,4096]{1,0:T(8,128)}), f32[64,256]{1,0:T(8,128)}) %reduce-scatter.5.cloned.1.call-update) | async-done | bytes 65552 | tf_op jit(solution)/shard_map/reduce_scatter | solution.py:113
  136.1 0.8 broadcast_divide_fusion
  136.9 0.1 fusion.72
  137.0 1.3 collective-permute-start
  138.3 1.3 collective-permute-start.1
  139.6 0.6 gather_fusion
  140.2 0.1 copy.18
  140.4 2.5 %collective-permute-done.1 = f32[64,15]{1,0:T(8,128)S(1)} collective-permute-done((f32[64,15]{1,0:T(8,128)S(1)}, f32[64,15]{1,0:T(8,128)S(1)}, u32[]{:S(2)}, u32[]{:S(2)}) %collective-permute-start.1) | collective-permute-done | bytes 3872 | tf_op jit(solution)/shard_map/ppermute | solution.py:28
  142.9 0.8 fusion.11
  143.7 2.5 %fusion.7 = f32[49,32,286]{2,0,1:T(8,128)S(1)} fusion(f32[49,15,1]{0,1,2:T(8,128)S(1)} %copy-done.2, f32[15,32,286]{2,1,0:T(8,128)S(1)} %fusion.11), kind=kOutput, calls=%fused_computation.12 | convolution fusion | flops 80720640 | bytes 2345852 | tf_op jit(solution)/shard_map/kj,jrc->krc/dot_general | solution.py:120
  146.2 23.3 %fusion = f32[49,32,256]{2,1,0:T(8,128)S(1)} fusion(f32[49,286,256]{2,0,1:T(8,128)} %fusion.2, f32[49,32,286]{2,0,1:T(8,128)S(1)} %fusion.7), kind=kOutput, calls=%fused_computation.1 | convolution fusion | flops 1377632256 | bytes 17749760 | tf_op jit(solution)/shard_map/krs,kso->kro/dot_general | solution.py:127
  169.5 0.6 broadcast_multiply_fusion
  170.1 0.7 slice_bitcast_fusion
  170.8 5.2 %fusion.3 = f32[16,32,256]{2,0,1:T(8,128)S(1)} fusion(f32[32,256,147]{1,0,2:T(8,128)S(1)} %slice_bitcast_fusion, f32[16,147]{0,1:T(8,128)S(1)} %reshape.229), kind=kOutput, calls=%fused_computation.5 | convolution fusion | flops 231211008 | bytes 5350592 | tf_op jit(solution)/shard_map/dot_general | solution.py:132
  176.0 0.3 copy.25
  176.3 21.2 %all_to_all.18 = f32[16,32,256]{2,1,0:T(8,128)S(1)} all-to-all(f32[16,32,256]{2,1,0:T(8,128)S(1)} %copy.25), channel_id=1, replica_groups=mesh['patch'=2,'epoch'=16] {'epoch'}, dimensions={0} | all-to-all | bytes 1048576 | tf_op jit(solution)/shard_map/all_to_all | solution.py:138
  197.6 0.9 subtract_multiply_fusion
  (73 shorter events, 0.6 us)
Async XLA Ops:
  6.5 133.1 %copy-start = (f32[16,49,3]{1,0,2:T(8,128)S(1)}, f32[16,49,3]{1,0,2:T(8,128)}, u32[]{:S(2)}) copy-start(f32[16,49,3]{1,0,2:T(8,128)} %param.8) | copy-start | bytes 28228
  6.5 5.5 %copy-start.3 = (f32[49]{0:T(128)S(1)}, f32[49]{0:T(128)}, u32[]{:S(2)}) copy-start(f32[49]{0:T(128)} %constant.101) | copy-start | bytes 592
  6.5 5.5 %copy-start.4 = (f32[49]{0:T(128)S(1)}, f32[49]{0:T(128)}, u32[]{:S(2)}) copy-start(f32[49]{0:T(128)} %constant.73) | copy-start | bytes 592
  6.5 5.6 %copy-start.5 = (f32[49]{0:T(128)S(1)}, f32[49]{0:T(128)}, u32[]{:S(2)}) copy-start(f32[49]{0:T(128)} %constant.75) | copy-start | bytes 592
  6.5 5.6 %copy-start.6 = (f32[49]{0:T(128)S(1)}, f32[49]{0:T(128)}, u32[]{:S(2)}) copy-start(f32[49]{0:T(128)} %constant.77) | copy-start | bytes 592
  6.6 5.6 %copy-start.7 = (f32[49]{0:T(128)S(1)}, f32[49]{0:T(128)}, u32[]{:S(2)}) copy-start(f32[49]{0:T(128)} %constant.79) | copy-start | bytes 592
  6.6 5.6 %copy-start.8 = (f32[49]{0:T(128)S(1)}, f32[49]{0:T(128)}, u32[]{:S(2)}) copy-start(f32[49]{0:T(128)} %constant.81) | copy-start | bytes 592
  6.6 5.6 %copy-start.9 = (f32[49]{0:T(128)S(1)}, f32[49]{0:T(128)}, u32[]{:S(2)}) copy-start(f32[49]{0:T(128)} %constant.83) | copy-start | bytes 592
  6.6 5.6 %copy-start.10 = (f32[49]{0:T(128)S(1)}, f32[49]{0:T(128)}, u32[]{:S(2)}) copy-start(f32[49]{0:T(128)} %constant.85) | copy-start | bytes 592
  6.6 5.6 %copy-start.11 = (f32[49]{0:T(128)S(1)}, f32[49]{0:T(128)}, u32[]{:S(2)}) copy-start(f32[49]{0:T(128)} %constant.87) | copy-start | bytes 592
  6.6 5.6 %copy-start.12 = (f32[49]{0:T(128)S(1)}, f32[49]{0:T(128)}, u32[]{:S(2)}) copy-start(f32[49]{0:T(128)} %constant.89) | copy-start | bytes 592
  6.6 5.6 %copy-start.13 = (f32[49]{0:T(128)S(1)}, f32[49]{0:T(128)}, u32[]{:S(2)}) copy-start(f32[49]{0:T(128)} %constant.91) | copy-start | bytes 592
  6.6 5.5 %copy-start.14 = (f32[49]{0:T(128)S(1)}, f32[49]{0:T(128)}, u32[]{:S(2)}) copy-start(f32[49]{0:T(128)} %constant.93) | copy-start | bytes 592
  6.7 5.5 %copy-start.15 = (f32[49]{0:T(128)S(1)}, f32[49]{0:T(128)}, u32[]{:S(2)}) copy-start(f32[49]{0:T(128)} %constant.95) | copy-start | bytes 592
  6.7 5.5 %copy-start.16 = (f32[49]{0:T(128)S(1)}, f32[49]{0:T(128)}, u32[]{:S(2)}) copy-start(f32[49]{0:T(128)} %constant.97) | copy-start | bytes 592
  6.7 5.5 %copy-start.17 = (f32[49]{0:T(128)S(1)}, f32[49]{0:T(128)}, u32[]{:S(2)}) copy-start(f32[49]{0:T(128)} %constant.99) | copy-start | bytes 592
  6.7 3.4 %copy-start.1 = (f32[1,64,4096]{2,1,0:T(8,128)S(1)}, f32[1,64,4096]{2,1,0:T(8,128)}, u32[]{:S(2)}) copy-start(f32[1,64,4096]{2,1,0:T(8,128)} %param.6) | copy-start | bytes 3145732
  6.7 4.9 %copy-start.18 = (s32[16]{0:T(128)S(1)}, s32[16]{0:T(128)}, u32[]{:S(2)}) copy-start(s32[16]{0:T(128)} %param.9) | copy-start | bytes 196
  6.7 68.9 %reduce-scatter.7.cloned.1.call-start = ((), (), s32[]{:S(2)}) async-start(), calls=%async_computation.4 | async-start | bytes 2228224
  9.9 126.2 %reduce-scatter.5.cloned.1.call-start = ((), (), s32[]{:S(2)}) async-start(), calls=%async_computation.3 | async-start | bytes 1114112 | tf_op jit(solution)/shard_map/reduce_scatter | solution.py:113
  22.1 121.6 %copy-start.2 = (f32[49,15,1]{0,1,2:T(8,128)S(1)}, f32[49,15,1]{0,1,2:T(8,128)}, u32[]{:S(2)}) copy-start(f32[49,15,1]{0,1,2:T(8,128)} %constant.102) | copy-start | bytes 8824
  137.0 3.4 %collective-permute-start = (f32[64,15]{1,0:T(8,128)S(1)}, f32[64,15]{1,0:T(8,128)S(1)}, u32[]{:S(2)}, u32[]{:S(2)}) collective-permute-start(f32[64,15]{1,0:T(8,128)S(1)} %get-tuple-element.5), channel_id=1, source_target_pairs={{0,1},{1,2},{2,3},{3,4},{4,5},{5,6},{6,7},{7,8},{8,9},{9,10},{10,1... | collective-permute-start | bytes 11528 | tf_op jit(solution)/shard_map/ppermute | solution.py:26
  138.3 4.6 %collective-permute-start.1 = (f32[64,15]{1,0:T(8,128)S(1)}, f32[64,15]{1,0:T(8,128)S(1)}, u32[]{:S(2)}, u32[]{:S(2)}) collective-permute-start(f32[64,15]{1,0:T(8,128)S(1)} %get-tuple-element.6), channel_id=1, source_target_pairs={{1,0},{2,1},{3,2},{4,3},{5,4},{6,5},{7,6},{8,7},{9,8},{10,9},{11,1... | collective-permute-start | bytes 11528 | tf_op jit(solution)/shard_map/ppermute | solution.py:28
Sparse Core Ops, SparseCore 0:
  11.3 64.2 reduce-scatter.6
  79.6 56.3 reduce-scatter.4
where the time goes:
time: 206 us; the launch traced here: 205 us
  waiting for transfers between devices  116 us (56%)
  matrix products  41.8 us (20%)
  blocking collectives  21.2 us (10%)
  between operations  13.9 us (7%)
  local copies, waits for them, and re-layouts  5.4 us (3%)
  other arithmetic  4.66 us (2%)
  starting transfers between devices  2.66 us (1%)
    reduce_scatter x1, waiting for transfers between devices, shards(): lax.psum_scatter(part_total, 'epoch', scatter_dimension=1, tiled=True)  59.5 us
    unnamed x3, waiting for transfers between devices  53.5 us
    dot_general x1, matrix products, shards(): jnp.einsum('krs,kso->kro', picked, horiz_mats, precision=lax.Precision.HI...  23.3 us
    all_to_all x1, blocking collectives, shards(): lax.all_to_all(models, 'epoch', split_axis=0, concat_axis=2, tiled=True)  21.2 us
    dot_general x1, matrix products, shards(): jnp.einsum('kd,dso->kso', horiz_filters, shift_table(horiz_filters.shape[...  9.87 us
    dot_general x1, matrix products, shards(): jnp.dot(coef_table, basis_images, precision=lax.Precision.HIGHEST, prefer...  5.15 us
  transfers between devices with their start and end apart: 4, of which 3 were waited for; matrix products, arithmetic and copies ran while one was open for 7% of the time, Pallas kernels for 0%

commit v1 on v0

--- a/solution.py
+++ b/solution.py
@@ -2,13 +2,19 @@
 
 import jax
 import jax.numpy as jnp
+import ml_dtypes
 import numpy as np
 from jax import lax
+from jax.experimental import pallas as pl
+from jax.experimental.pallas import tpu as pltpu
 from jax.sharding import PartitionSpec as P
 
 HALF = 15
 MARGIN = 16
 BAND = 64
+KERNELS = 49
+POLY = 3
+LANES = 128
 
 
 gauss_widths = (1.5, 3.0, 6.0)
@@ -140,6 +146,319 @@
     return valid_mask[:, MARGIN : MARGIN + rows_out] * (centre - model_image)
 
 
+def filter_values():
+    offsets = np.arange(-HALF, HALF + 1).astype(np.float64)
+    groups = []
+    for spread, degree in zip(gauss_widths, gauss_degrees):
+        envelope = np.exp(-offsets * offsets / (2.0 * spread * spread)) / (math.sqrt(2.0 * math.pi) * spread)
+        groups.append([envelope * (offsets / spread) ** power for power in range(degree + 1)])
+    return groups
+
+
+def split_constant(values):
+    values = values.astype(np.float32)
+    high = values.astype(ml_dtypes.bfloat16)
+    low = (values - high.astype(np.float32)).astype(ml_dtypes.bfloat16)
+    return high, low
+
+
+def kernel_constants(rows_out, padded_rows):
+    groups = filter_values()
+    vert = np.zeros((len(groups), rows_out, 8, padded_rows))
+    for g, filters in enumerate(groups):
+        for j, taps in enumerate(filters):
+            for r in range(rows_out):
+                start = r + MARGIN - HALF
+                vert[g, r, j, start : start + taps.shape[0]] = taps
+    vert = vert.reshape(len(groups) * rows_out * 8, padded_rows)
+    high, low = split_constant(vert)
+    vert_stack = np.concatenate([high, high, low], axis=1)
+    flat = [taps for filters in groups for taps in filters]
+    horiz = np.zeros((2 * LANES, len(flat), LANES))
+    for h, taps in enumerate(flat):
+        for o in range(LANES):
+            start = o + LANES // 2 - HALF
+            horiz[start : start + taps.shape[0], h, o] = taps
+    horiz_stack = np.stack(split_constant(horiz.reshape(2 * LANES, len(flat) * LANES)))
+    place = np.zeros((KERNELS, LANES), np.float32)
+    index, base = 0, 0
+    for degree in gauss_degrees:
+        for a in range(degree + 1):
+            for b in range(degree + 1 - a):
+                place[index, (base + b) * 8 + a] = 1.0
+                index += 1
+        base += degree + 1
+    return vert_stack, horiz_stack, place
+
+
+def split(values):
+    high = values.astype(jnp.bfloat16)
+    return high, (values - high.astype(jnp.float32)).astype(jnp.bfloat16)
+
+
+def dot32(a, b):
+    return jnp.dot(a, b, preferred_element_type=jnp.float32)
+
+
+def exact(a, b):
+    return jnp.dot(a, b, precision=lax.Precision.HIGHEST, preferred_element_type=jnp.float32)
+
+
+def strip_kernel(
+    image, words, coef, order, place, vert_hbm, horiz_hbm, out,
+    sums, got_core, got_y, got_z, ext, valid, vert, horiz, v_high, v_low, conv, mix, models, got,
+    const_sem, send_core, recv_core, send_y, recv_y, send_z, recv_z, send_halo, recv_halo, send_model, recv_model,
+):
+    count = 16
+    zs = count // 4
+    slab = 2 * LANES
+    me = lax.axis_index("epoch")
+    k = lax.rem(me, 2)
+    y = lax.rem(me // 2, 2)
+    z = me // 4
+
+    def remote(src, dst, ssem, rsem, device):
+        return pltpu.make_async_remote_copy(
+            src_ref=src, dst_ref=dst, send_sem=ssem, recv_sem=rsem,
+            device_id={"epoch": device}, device_id_type=pl.DeviceIdType.MESH,
+        )
+
+    barrier = pltpu.get_barrier_semaphore()
+    for d in range(1, count):
+        pl.semaphore_signal(
+            barrier, inc=1, device_id={"epoch": lax.rem(me + d, count)}, device_id_type=pl.DeviceIdType.MESH
+        )
+    copy_vert = pltpu.make_async_copy(vert_hbm, vert, const_sem.at[0])
+    copy_horiz = pltpu.make_async_copy(horiz_hbm, horiz, const_sem.at[1])
+    copy_vert.start()
+    copy_horiz.start()
+
+    lane = lax.broadcasted_iota(jnp.int32, (8, LANES), 1)
+    place_bit = lane & 31
+    for q in range(count):
+        for half in range(2):
+            t = q * 2 + half
+            word = jnp.where(
+                lane < 64,
+                jnp.where(lane < 32, words[4 * t], words[4 * t + 1]),
+                jnp.where(lane < 96, words[4 * t + 2], words[4 * t + 3]),
+            )
+            bits = (jnp.right_shift(word, place_bit) & 1).astype(jnp.float32)
+            valid[:, t * LANES : (t + 1) * LANES] = bits
+            spot = sums.at[q % 2, (q // 2) % 2, q // 4]
+            for s in range(0, 64, 8):
+                spot[s : s + 8, half * LANES : (half + 1) * LANES] = (
+                    bits * image[0, s : s + 8, t * LANES : (t + 1) * LANES]
+                )
+            spot[0:1, half * LANES : (half + 1) * LANES] = bits[0:1]
+    pl.semaphore_wait(barrier, count - 1)
+
+    core_copies = []
+    for h, yy in enumerate((1 - y, y)):
+        copy = remote(
+            sums.at[1 - k, yy], got_core.at[yy], send_core.at[h], recv_core.at[h], me + 1 - 2 * k
+        )
+        copy.start()
+        core_copies.append(copy)
+    core_copies[0].wait_recv()
+    ring = [lax.rem(z + d, zs) for d in (2, 1, 3, 0)]
+    y_copies = []
+    for zz in ring:
+        sums[k, 1 - y, zz] = sums[k, 1 - y, zz] + got_core[1 - y, zz]
+        copy = remote(sums.at[k, 1 - y, zz], got_y.at[zz], send_y.at[zz], recv_y.at[zz], me + 2 - 4 * y)
+        copy.start()
+        y_copies.append(copy)
+    core_copies[1].wait_recv()
+    for zz in ring:
+        sums[k, y, zz] = sums[k, y, zz] + got_core[y, zz]
+
+    slots = lax.broadcasted_iota(jnp.int32, (count, count), 1)
+    pick = (slots == order[...]).astype(jnp.float32)
+    for p in range(POLY):
+        table = exact(exact(pick, coef[p]), place[...])
+        high, low = split(table)
+        rows = slice(p * count, (p + 1) * count)
+        mix[rows, :LANES] = high
+        mix[rows, LANES:] = high
+        rows = slice((POLY + p) * count, (POLY + p + 1) * count)
+        mix[rows, :LANES] = low
+        mix[rows, LANES:] = jnp.zeros_like(low)
+
+    z_copies = []
+    for zz, copy in zip(ring, y_copies):
+        copy.wait_recv()
+        sums[k, y, zz] = sums[k, y, zz] + got_y[zz]
+        if len(z_copies) < zs - 1:
+            sent = remote(
+                sums.at[k, y, zz], got_z.at[z], send_z.at[zz], recv_z.at[z], zz * 4 + lax.rem(me, 4)
+            )
+            sent.start()
+            z_copies.append(sent)
+    copy_vert.wait()
+    copy_horiz.wait()
+    for zz in ring[:-1]:
+        remote(sums.at[k, y, zz], got_z.at[zz], send_z.at[zz], recv_z.at[zz], me).wait_recv()
+    total = sums[k, y, z]
+    for zz in ring[:-1]:
+        total = total + got_z[zz]
+    ext[:, LANES : 3 * LANES] = total / jnp.maximum(total[0:1], 1.0)
+
+    left = lax.rem(me + count - 1, count)
+    right = lax.rem(me + 1, count)
+    halo = [
+        remote(ext.at[:, LANES : 2 * LANES], ext.at[:, 3 * LANES :], send_halo.at[0], recv_halo.at[0], left),
+        remote(ext.at[:, 2 * LANES : 3 * LANES], ext.at[:, :LANES], send_halo.at[1], recv_halo.at[1], right),
+    ]
+    for copy in halo:
+        copy.start()
+    for copy in halo:
+        copy.wait_recv()
+    first = jnp.where(me > 0, ext[:, :LANES], 0.0)
+    last = jnp.where(me < count - 1, ext[:, 3 * LANES :], 0.0)
+    joined = jnp.concatenate([first, ext[:, LANES : 3 * LANES], last], axis=1)
+    half = LANES // 2
+    windows = jnp.concatenate([joined[:, half : half + slab], joined[:, LANES + half : LANES + half + slab]], axis=1)
+    high, low = split(windows)
+    stacked = jnp.concatenate([high, low, high], axis=0)
+    groups = len(gauss_degrees)
+    block = 256
+    for g in range(groups):
+        rows = slice(g * block, (g + 1) * block)
+        made = dot32(vert[rows, :], stacked)
+        high, low = split(made)
+        v_high[rows, :] = high
+        v_low[rows, :] = low
+    for w in range(2):
+        base = 0
+        for g, degree in enumerate(gauss_degrees):
+            rows = slice(g * block, (g + 1) * block)
+            cols = slice(w * slab, (w + 1) * slab)
+            outs = slice(base * LANES, (base + degree + 1) * LANES)
+            conv[w, :, outs] = (
+                dot32(v_high[rows, cols], horiz[0, :, outs])
+                + dot32(v_low[rows, cols], horiz[0, :, outs])
+                + dot32(v_high[rows, cols], horiz[1, :, outs])
+            )
+            base += degree + 1
+
+    column = me * slab + lax.broadcasted_iota(jnp.int32, (count, slab), 1)
+    across = (2.0 * column.astype(jnp.float32) + 1.0) / (count * slab) - 1.0
+    pairs = 15
+    rows_out = 32
+
+    def model_rows(blk, carry):
+        for i in range(8):
+            r = blk * 8 + i
+            start = pl.multiple_of(r * 8, 8)
+            sides = []
+            for w in range(2):
+                line = conv[w, pl.ds(start, 8), :]
+                pieces = [line[:, h * LANES : (h + 1) * LANES] for h in range(pairs)]
+                pieces.append(jnp.zeros((8, LANES), jnp.float32))
+                sides.append(jnp.concatenate(pieces, axis=0))
+            high, low = split(jnp.concatenate(sides, axis=1))
+            made = dot32(mix[...], jnp.concatenate([high, low], axis=0))
+            made = made[: POLY * count] + made[POLY * count :]
+            down = (2.0 * lax.convert_element_type(r, jnp.float32) + 1.0) / rows_out - 1.0
+            models[:, r, :] = made[:count] + across * made[count : 2 * count] + down * made[2 * count :]
+        start = pl.multiple_of(blk * 8, 8)
+        for d in ORDER:
+            peer = lax.rem(me + d, count)
+            remote(
+                models.at[peer, pl.ds(start, 8)], got.at[me, pl.ds(start, 8)],
+                send_model.at[blk, peer], recv_model.at[blk, me], peer,
+            ).start()
+        return carry
+
+    lax.fori_loop(0, rows_out // 8, model_rows, 0)
+
+    def finish(q, source):
+        start = pl.multiple_of(q * slab, slab)
+        seen = valid[:, pl.ds(start, slab)]
+        for s in range(0, rows_out, 8):
+            out[0, s : s + 8, pl.ds(start, slab)] = seen * (
+                image[0, MARGIN + s : MARGIN + s + 8, pl.ds(start, slab)] - source[q, s : s + 8, :]
+            )
+
+    finish(me, models)
+    for d in ORDER:
+        q = lax.rem(me + count - d, count)
+        for blk in range(rows_out // 8):
+            rows = pl.ds(blk * 8, 8)
+            remote(
+                models.at[q, rows], got.at[q, rows], send_model.at[blk, q], recv_model.at[blk, q], q
+            ).wait_recv()
+        finish(q, got)
+
+    for copy in core_copies + y_copies + z_copies + halo:
+        copy.wait_send()
+    for d in ORDER:
+        peer = lax.rem(me + d, count)
+        for blk in range(rows_out // 8):
+            rows = pl.ds(blk * 8, 8)
+            remote(
+                models.at[peer, rows], got.at[me, rows], send_model.at[blk, peer], recv_model.at[blk, me], peer
+            ).wait_send()
+
+
+ORDER = (8, 7, 9, 6, 10, 5, 11, 4, 12, 3, 13, 2, 14, 1, 15)
+
+
+def strip(epoch_images, mask_words, coefficients, epoch_order):
+    vert, horiz, place = kernel_constants(32, 64)
+    vmem = pl.BlockSpec(memory_space=pltpu.VMEM)
+    smem = pl.BlockSpec(memory_space=pltpu.SMEM)
+    anywhere = pl.BlockSpec(memory_space=pl.ANY)
+    f32 = jnp.float32
+    bf16 = jnp.bfloat16
+    dma = pltpu.SemaphoreType.DMA
+    return pl.pallas_call(
+        strip_kernel,
+        out_shape=jax.ShapeDtypeStruct((1, 32, 4096), f32),
+        in_specs=[vmem, smem, vmem, vmem, vmem, anywhere, anywhere],
+        out_specs=vmem,
+        scratch_shapes=[
+            pltpu.VMEM((2, 2, 4, 64, 256), f32),
+            pltpu.VMEM((2, 4, 64, 256), f32),
+            pltpu.VMEM((4, 64, 256), f32),
+            pltpu.VMEM((4, 64, 256), f32),
+            pltpu.VMEM((64, 512), f32),
+            pltpu.VMEM((8, 4096), f32),
+            pltpu.VMEM(vert.shape, bf16),
+            pltpu.VMEM(horiz.shape, bf16),
+            pltpu.VMEM((768, 512), bf16),
+            pltpu.VMEM((768, 512), bf16),
+            pltpu.VMEM((2, 256, 15 * LANES), f32),
+            pltpu.VMEM((96, 256), bf16),
+            pltpu.VMEM((16, 32, 256), f32),
+            pltpu.VMEM((16, 32, 256), f32),
+            dma((2,)),
+            dma((2,)),
+            dma((2,)),
+            dma((4,)),
+            dma((4,)),
+            dma((4,)),
+            dma((4,)),
+            dma((2,)),
+            dma((2,)),
+            dma((4, 16)),
+            dma((4, 16)),
+        ],
+        compiler_params=pltpu.CompilerParams(
+            collective_id=0, has_side_effects=True, vmem_limit_bytes=40 * 1024 * 1024
+        ),
+        cost_estimate=pl.CostEstimate(flops=2 * 10**9, bytes_accessed=4 * 10**6, transcendentals=0),
+    )(
+        epoch_images,
+        mask_words.reshape(-1),
+        jnp.transpose(coefficients, (2, 0, 1)),
+        epoch_order.reshape(-1, 1),
+        jnp.asarray(place),
+        jnp.asarray(vert),
+        jnp.asarray(horiz),
+    )
+
+
 def solution(mesh):
     placed = (
         P(("patch", "epoch"), None, None),
@@ -147,8 +466,9 @@
         P("patch", None, None),
         P("patch"),
     )
+    body = strip if mesh.shape["epoch"] == 16 else shards
     return jax.shard_map(
-        shards,
+        body,
         mesh=mesh,
         in_specs=placed,
         out_specs=P(("patch", "epoch"), None, None),

time: 206 us -> 45.3 us (0.22)
  waiting for transfers between devices: 116 us -> 0 us
  matrix products: 41.8 us -> 0 us
  Pallas kernels: 0 us -> 37.5 us
  blocking collectives: 21.2 us -> 0 us
  between operations: 13.9 us -> 0.02 us
  other arithmetic: 4.66 us -> 0 us
  starting transfers between devices: 2.66 us -> 0 us
    reduce_scatter x1 -> x0, waiting for transfers between devices: 59.5 us -> none  [shards(): lax.psum_scatter(part_total, 'epoch', scatter_dimension=1, tiled=True)]
    unnamed x3 -> x0, waiting for transfers between devices: 53.5 us -> none
    dot_general x6 -> x0, matrix products: 41.8 us -> none  [the longest x1 23.3 us: shards(): jnp.einsum('krs,kso->kro', picked, horiz_mats, precision=lax.Precision.HI...]
    pallas_call x0 -> x1, Pallas kernels: none -> 37.5 us  [strip(): pl.pallas_call(strip_kernel, out_shape=jax.ShapeDtypeStruct((1, 32, 4096)...]
    all_to_all x1 -> x0, blocking collectives: 21.2 us -> none  [shards(): lax.all_to_all(models, 'epoch', split_axis=0, concat_axis=2, tiled=True)]
    unnamed x40 -> x13, local copies, waits for them, and re-layouts: 2.16 us -> 6.7 us
    ppermute x2 -> x0, starting transfers between devices: 2.58 us -> none  [the longest x1 1.29 us: extended(): lax.ppermute(head, axis, [((i + 1) % count, i) for i in range(ends)])]
    ppermute x2 -> x0, waiting for transfers between devices: 2.51 us -> none  [the longest x1 2.51 us: extended(): lax.ppermute(head, axis, [((i + 1) % count, i) for i in range(ends)])]
  transfers between devices with their start and end apart: 4 -> 0, of which waited for: 3 -> 0; matrix products, arithmetic and copies ran while one was open for 7% -> 0% of each run, Pallas kernels for 0% -> 0%
where the time goes in v1:
time: 45.3 us; the launch traced here: 44.9 us
  Pallas kernels  37.5 us (83%)
  local copies, waits for them, and re-layouts  7.43 us (16%)
    pallas_call x1, Pallas kernels, strip(): pl.pallas_call(strip_kernel, out_shape=jax.ShapeDtypeStruct((1, 32, 4096)...  37.5 us
    unnamed x13, local copies, waits for them, and re-layouts  6.7 us

profile of v1, /device:TPU:0, one launch (start us, length us, event | category | flops | bytes accessed | tf_op | source)
XLA Modules:
  0.0 44.9 jit_solution(15991177660151119573)
XLA Ops:
  0.0 0.7 %copy.8.order = s32[16,1]{1,0:T(8,128)S(1)} copy(s32[16,1]{0,1:T(1,128)} %bitcast.5) | data formatting | bytes 128 | tf_op jit(solution)/shard_map/reshape | solution.py:455
  0.7 0.0 copy-start
  0.7 1.2 %copy-done = f32[1,64,4096]{2,1,0:T(8,128)S(1)} copy-done((f32[1,64,4096]{2,1,0:T(8,128)S(1)}, f32[1,64,4096]{2,1,0:T(8,128)}, u32[]{:S(2)}) %copy-start) | copy-done | bytes 1048600
  2.0 0.0 copy-start.1
  2.0 0.7 %copy-done.1 = f32[16,49,3]{1,0,2:T(8,128)S(1)} copy-done((f32[16,49,3]{1,0,2:T(8,128)S(1)}, f32[16,49,3]{1,0,2:T(8,128)}, u32[]{:S(2)}) %copy-start.1) | copy-done | bytes 9432
  2.7 0.0 copy-start.2
  2.7 0.7 %copy-done.2 = s32[1,1,128]{2,1,0:T(1,128)S(1)} copy-done((s32[1,1,128]{2,1,0:T(1,128)S(1)}, s32[1,1,128]{2,1,0:T(1,128)}, u32[]{:S(2)}) %copy-start.2) | copy-done | bytes 536
  3.4 0.0 copy-start.3
  3.4 1.5 %copy-done.3 = bf16[2,256,1920]{2,1,0:T(8,128)(2,1)S(1)} copy-done((bf16[2,256,1920]{2,1,0:T(8,128)(2,1)S(1)}, bf16[2,256,1920]{2,1,0:T(8,128)(2,1)}, u32[]{:S(2)}) %copy-start.3) | copy-done | bytes 1966104
  4.9 0.0 copy-start.4
  4.9 1.0 %copy-done.4 = bf16[768,192]{1,0:T(8,128)(2,1)S(1)} copy-done((bf16[768,192]{1,0:T(8,128)(2,1)S(1)}, bf16[768,192]{1,0:T(8,128)(2,1)}, u32[]{:S(2)}) %copy-start.4) | copy-done | bytes 294936
  5.9 0.0 copy-start.5
  5.9 0.7 %copy-done.5 = f32[49,128]{1,0:T(8,128)S(1)} copy-done((f32[49,128]{1,0:T(8,128)S(1)}, f32[49,128]{1,0:T(8,128)}, u32[]{:S(2)}) %copy-start.5) | copy-done | bytes 25112
  6.6 37.5 %shard_map.73 = f32[1,32,4096]{2,1,0:T(8,128)S(1)} custom-call(f32[1,64,4096]{2,1,0:T(8,128)S(1)} %copy-done, s32[128]{0:T(128)S(1)} %bitcast.4, f32[3,16,49]{2,1,0:T(8,128)S(1)} %bitcast.3, s32[16,1]{1,0:T(8,128)S(1)} %copy.8.order, f32[49,128]{1,0:T(8,128)S(1)} %copy-done.5, bf16[768,192]{1,0:T(8,128)(2,1)S(1)} %copy-done.4, ...), custom_call_target="tpu_custom_call" | custom-call | flops 2000000000 | bytes 4000000 | tf_op jit(solution)/shard_map/pallas_call | solution.py:415
  44.2 0.8 %copy.10 = f32[1,32,4096]{2,1,0:T(8,128)} copy(f32[1,32,4096]{2,1,0:T(8,128)S(1)} %shard_map.73) | data formatting | bytes 1048576
Async XLA Ops:
  0.7 1.2 %copy-start = (f32[1,64,4096]{2,1,0:T(8,128)S(1)}, f32[1,64,4096]{2,1,0:T(8,128)}, u32[]{:S(2)}) copy-start(f32[1,64,4096]{2,1,0:T(8,128)} %image.1) | copy-start | bytes 3145732
  2.0 0.7 %copy-start.1 = (f32[16,49,3]{1,0,2:T(8,128)S(1)}, f32[16,49,3]{1,0,2:T(8,128)}, u32[]{:S(2)}) copy-start(f32[16,49,3]{1,0,2:T(8,128)} %param.9) | copy-start | bytes 28228
  2.7 0.7 %copy-start.2 = (s32[1,1,128]{2,1,0:T(1,128)S(1)}, s32[1,1,128]{2,1,0:T(1,128)}, u32[]{:S(2)}) copy-start(s32[1,1,128]{2,1,0:T(1,128)} %param.8) | copy-start | bytes 1540
  3.4 1.5 %copy-start.3 = (bf16[2,256,1920]{2,1,0:T(8,128)(2,1)S(1)}, bf16[2,256,1920]{2,1,0:T(8,128)(2,1)}, u32[]{:S(2)}) copy-start(bf16[2,256,1920]{2,1,0:T(8,128)(2,1)} %constant.8.clone.horiz_hbm) | copy-start | bytes 5898244
  4.9 1.0 %copy-start.4 = (bf16[768,192]{1,0:T(8,128)(2,1)S(1)}, bf16[768,192]{1,0:T(8,128)(2,1)}, u32[]{:S(2)}) copy-start(bf16[768,192]{1,0:T(8,128)(2,1)} %constant.7.clone.vert_hbm) | copy-start | bytes 884740
  5.9 0.7 %copy-start.5 = (f32[49,128]{1,0:T(8,128)S(1)}, f32[49,128]{1,0:T(8,128)}, u32[]{:S(2)}) copy-start(f32[49,128]{1,0:T(8,128)} %constant.6.clone.place) | copy-start | bytes 75268

commit v2 on v1

--- a/solution.py
+++ b/solution.py
@@ -170,9 +170,10 @@
             for r in range(rows_out):
                 start = r + MARGIN - HALF
                 vert[g, r, j, start : start + taps.shape[0]] = taps
-    vert = vert.reshape(len(groups) * rows_out * 8, padded_rows)
+    vert = vert.reshape(len(groups), rows_out // 8, 64, padded_rows).swapaxes(0, 1)
+    vert = vert.reshape(rows_out // 8, len(groups) * 64, padded_rows)
     high, low = split_constant(vert)
-    vert_stack = np.concatenate([high, high, low], axis=1)
+    vert_stack = np.concatenate([high, high, low], axis=2)
     flat = [taps for filters in groups for taps in filters]
     horiz = np.zeros((2 * LANES, len(flat), LANES))
     for h, taps in enumerate(flat):
@@ -205,9 +206,9 @@
 
 
 def strip_kernel(
-    image, words, coef, order, place, vert_hbm, horiz_hbm, out,
-    sums, got_core, got_y, got_z, ext, valid, vert, horiz, v_high, v_low, conv, mix, models, got,
-    const_sem, send_core, recv_core, send_y, recv_y, send_z, recv_z, send_halo, recv_halo, send_model, recv_model,
+    image_hbm, words_hbm, coef_hbm, order_hbm, place_hbm, vert_hbm, horiz_hbm, out,
+    image, words, coef, order, place, sums, got_core, got_y, got_z, ext, valid, vert, horiz, conv, mix, models, got,
+    load_sem, const_sem, send_core, recv_core, send_y, recv_y, send_z, recv_z, send_halo, recv_halo, send_model, recv_model,
 ):
     count = 16
     zs = count // 4
@@ -223,19 +224,26 @@
             device_id={"epoch": device}, device_id_type=pl.DeviceIdType.MESH,
         )
 
+    words_load = pltpu.make_async_copy(words_hbm, words, load_sem.at[0])
+    words_load.start()
+    loads = []
+    for c in range(4):
+        part = pl.ds(c * 1024, 1024)
+        load = pltpu.make_async_copy(image_hbm.at[:, :, part], image.at[:, :, part], load_sem.at[1 + c])
+        load.start()
+        loads.append(load)
     barrier = pltpu.get_barrier_semaphore()
     for d in range(1, count):
         pl.semaphore_signal(
             barrier, inc=1, device_id={"epoch": lax.rem(me + d, count)}, device_id_type=pl.DeviceIdType.MESH
         )
-    copy_vert = pltpu.make_async_copy(vert_hbm, vert, const_sem.at[0])
-    copy_horiz = pltpu.make_async_copy(horiz_hbm, horiz, const_sem.at[1])
-    copy_vert.start()
-    copy_horiz.start()
 
     lane = lax.broadcasted_iota(jnp.int32, (8, LANES), 1)
     place_bit = lane & 31
+    words_load.wait()
     for q in range(count):
+        if q % 4 == 0:
+            loads[q // 4].wait()
         for half in range(2):
             t = q * 2 + half
             word = jnp.where(
@@ -260,6 +268,12 @@
         )
         copy.start()
         core_copies.append(copy)
+    constants = []
+    sources = (order_hbm, coef_hbm, place_hbm, vert_hbm, horiz_hbm)
+    for c, (src, dst) in enumerate(zip(sources, (order, coef, place, vert, horiz))):
+        load = pltpu.make_async_copy(src, dst, const_sem.at[c])
+        load.start()
+        constants.append(load)
     core_copies[0].wait_recv()
     ring = [lax.rem(z + d, zs) for d in (2, 1, 3, 0)]
     y_copies = []
@@ -273,7 +287,13 @@
         sums[k, y, zz] = sums[k, y, zz] + got_core[y, zz]
 
     slots = lax.broadcasted_iota(jnp.int32, (count, count), 1)
-    pick = (slots == order[...]).astype(jnp.float32)
+    for load in constants:
+        load.wait()
+    rows = lax.broadcasted_iota(jnp.int32, (count, count), 0)
+    held = jnp.zeros((count, count), jnp.int32)
+    for e in range(count):
+        held = jnp.where(rows == e, order[e], held)
+    pick = (slots == held).astype(jnp.float32)
     for p in range(POLY):
         table = exact(exact(pick, coef[p]), place[...])
         high, low = split(table)
@@ -294,8 +314,6 @@
             )
             sent.start()
             z_copies.append(sent)
-    copy_vert.wait()
-    copy_horiz.wait()
     for zz in ring[:-1]:
         remote(sums.at[k, y, zz], got_z.at[zz], send_z.at[zz], recv_z.at[zz], me).wait_recv()
     total = sums[k, y, z]
@@ -320,40 +338,27 @@
     windows = jnp.concatenate([joined[:, half : half + slab], joined[:, LANES + half : LANES + half + slab]], axis=1)
     high, low = split(windows)
     stacked = jnp.concatenate([high, low, high], axis=0)
-    groups = len(gauss_degrees)
-    block = 256
-    for g in range(groups):
-        rows = slice(g * block, (g + 1) * block)
-        made = dot32(vert[rows, :], stacked)
-        high, low = split(made)
-        v_high[rows, :] = high
-        v_low[rows, :] = low
-    for w in range(2):
-        base = 0
-        for g, degree in enumerate(gauss_degrees):
-            rows = slice(g * block, (g + 1) * block)
-            cols = slice(w * slab, (w + 1) * slab)
-            outs = slice(base * LANES, (base + degree + 1) * LANES)
-            conv[w, :, outs] = (
-                dot32(v_high[rows, cols], horiz[0, :, outs])
-                + dot32(v_low[rows, cols], horiz[0, :, outs])
-                + dot32(v_high[rows, cols], horiz[1, :, outs])
-            )
-            base += degree + 1
-
     column = me * slab + lax.broadcasted_iota(jnp.int32, (count, slab), 1)
     across = (2.0 * column.astype(jnp.float32) + 1.0) / (count * slab) - 1.0
     pairs = 15
     rows_out = 32
 
     def model_rows(blk, carry):
+        made = dot32(vert[blk], stacked)
+        base = 0
+        for g, degree in enumerate(gauss_degrees):
+            rows = made[g * 64 : (g + 1) * 64]
+            high, low = split(jnp.concatenate([rows[:, :slab], rows[:, slab:]], axis=0))
+            outs = slice(base * LANES, (base + degree + 1) * LANES)
+            both = dot32(jnp.concatenate([high, low], axis=0), horiz[0, :, outs])
+            conv[:, outs] = both[:LANES] + both[LANES:] + dot32(high, horiz[1, :, outs])
+            base += degree + 1
         for i in range(8):
             r = blk * 8 + i
-            start = pl.multiple_of(r * 8, 8)
             sides = []
             for w in range(2):
-                line = conv[w, pl.ds(start, 8), :]
-                pieces = [line[:, h * LANES : (h + 1) * LANES] for h in range(pairs)]
+                line = slice(w * 64 + i * 8, w * 64 + i * 8 + 8)
+                pieces = [conv[line, h * LANES : (h + 1) * LANES] for h in range(pairs)]
                 pieces.append(jnp.zeros((8, LANES), jnp.float32))
                 sides.append(jnp.concatenate(pieces, axis=0))
             high, low = split(jnp.concatenate(sides, axis=1))
@@ -407,17 +412,21 @@
 def strip(epoch_images, mask_words, coefficients, epoch_order):
     vert, horiz, place = kernel_constants(32, 64)
     vmem = pl.BlockSpec(memory_space=pltpu.VMEM)
-    smem = pl.BlockSpec(memory_space=pltpu.SMEM)
-    anywhere = pl.BlockSpec(memory_space=pl.ANY)
+    hbm = pl.BlockSpec(memory_space=pltpu.HBM)
     f32 = jnp.float32
     bf16 = jnp.bfloat16
     dma = pltpu.SemaphoreType.DMA
     return pl.pallas_call(
         strip_kernel,
         out_shape=jax.ShapeDtypeStruct((1, 32, 4096), f32),
-        in_specs=[vmem, smem, vmem, vmem, vmem, anywhere, anywhere],
+        in_specs=[hbm] * 7,
         out_specs=vmem,
         scratch_shapes=[
+            pltpu.VMEM((1, 64, 4096), f32),
+            pltpu.SMEM((128,), jnp.int32),
+            pltpu.VMEM((3, 16, 49), f32),
+            pltpu.SMEM((16,), jnp.int32),
+            pltpu.VMEM(place.shape, f32),
             pltpu.VMEM((2, 2, 4, 64, 256), f32),
             pltpu.VMEM((2, 4, 64, 256), f32),
             pltpu.VMEM((4, 64, 256), f32),
@@ -426,13 +435,12 @@
             pltpu.VMEM((8, 4096), f32),
             pltpu.VMEM(vert.shape, bf16),
             pltpu.VMEM(horiz.shape, bf16),
-            pltpu.VMEM((768, 512), bf16),
-            pltpu.VMEM((768, 512), bf16),
-            pltpu.VMEM((2, 256, 15 * LANES), f32),
+            pltpu.VMEM((128, 15 * LANES), f32),
             pltpu.VMEM((96, 256), bf16),
             pltpu.VMEM((16, 32, 256), f32),
             pltpu.VMEM((16, 32, 256), f32),
-            dma((2,)),
+            dma((5,)),
+            dma((5,)),
             dma((2,)),
             dma((2,)),
             dma((4,)),
@@ -452,7 +460,7 @@
         epoch_images,
         mask_words.reshape(-1),
         jnp.transpose(coefficients, (2, 0, 1)),
-        epoch_order.reshape(-1, 1),
+        epoch_order,
         jnp.asarray(place),
         jnp.asarray(vert),
         jnp.asarray(horiz),

time: 45.3 us -> 43.5 us (0.960)
  Pallas kernels: 37.5 us -> 35.7 us
    pallas_call x1, Pallas kernels: 37.5 us -> 35.7 us  [strip(): pl.pallas_call(strip_kernel, out_shape=jax.ShapeDtypeStruct((1, 32, 4096)...]
    reshape x1 -> x0, local copies, waits for them, and re-layouts: 0.73 us -> none  [strip(): epoch_order.reshape(-1, 1)]
    unnamed x13 -> x15, local copies, waits for them, and re-layouts: 6.7 us -> 7.35 us
where the time goes in v2:
time: 43.5 us; the launch traced here: 43.1 us
  Pallas kernels  35.7 us (82%)
  local copies, waits for them, and re-layouts  7.35 us (17%)
    pallas_call x1, Pallas kernels, strip(): pl.pallas_call(strip_kernel, out_shape=jax.ShapeDtypeStruct((1, 32, 4096)...  35.7 us
    unnamed x15, local copies, waits for them, and re-layouts  7.35 us

profile of v2, /device:TPU:0, one launch (start us, length us, event | category | flops | bytes accessed | tf_op | source)
XLA Modules:
  0.0 43.1 jit_solution(2158445272771089928)
XLA Ops:
  0.0 0.0 copy-start
  0.0 1.2 %copy-done = f32[1,64,4096]{2,1,0:T(8,128)S(1)} copy-done((f32[1,64,4096]{2,1,0:T(8,128)S(1)}, f32[1,64,4096]{2,1,0:T(8,128)}, u32[]{:S(2)}) %copy-start) | copy-done | bytes 1048600
  1.2 0.0 copy-start.1
  1.2 0.7 %copy-done.1 = f32[16,49,3]{1,0,2:T(8,128)S(1)} copy-done((f32[16,49,3]{1,0,2:T(8,128)S(1)}, f32[16,49,3]{1,0,2:T(8,128)}, u32[]{:S(2)}) %copy-start.1) | copy-done | bytes 9432
  2.0 0.0 copy-start.2
  2.0 0.7 %copy-done.2 = s32[1,1,128]{2,1,0:T(1,128)S(1)} copy-done((s32[1,1,128]{2,1,0:T(1,128)S(1)}, s32[1,1,128]{2,1,0:T(1,128)}, u32[]{:S(2)}) %copy-start.2) | copy-done | bytes 536
  2.6 0.0 copy-start.3
  2.6 0.7 %copy-done.3 = s32[16]{0:T(128)S(1)} copy-done((s32[16]{0:T(128)S(1)}, s32[16]{0:T(128)}, u32[]{:S(2)}) %copy-start.3) | copy-done | bytes 88
  3.3 0.0 copy-start.4
  3.3 1.5 %copy-done.4 = bf16[2,256,1920]{2,1,0:T(8,128)(2,1)S(1)} copy-done((bf16[2,256,1920]{2,1,0:T(8,128)(2,1)S(1)}, bf16[2,256,1920]{2,1,0:T(8,128)(2,1)}, u32[]{:S(2)}) %copy-start.4) | copy-done | bytes 1966104
  4.8 0.0 copy-start.5
  4.8 1.0 %copy-done.5 = bf16[4,192,192]{2,1,0:T(8,128)(2,1)S(1)} copy-done((bf16[4,192,192]{2,1,0:T(8,128)(2,1)S(1)}, bf16[4,192,192]{2,1,0:T(8,128)(2,1)}, u32[]{:S(2)}) %copy-start.5) | copy-done | bytes 294936
  5.8 0.0 copy-start.6
  5.8 0.7 %copy-done.6 = f32[49,128]{1,0:T(8,128)S(1)} copy-done((f32[49,128]{1,0:T(8,128)S(1)}, f32[49,128]{1,0:T(8,128)}, u32[]{:S(2)}) %copy-start.6) | copy-done | bytes 25112
  6.6 35.7 %shard_map.73 = f32[1,32,4096]{2,1,0:T(8,128)S(1)} custom-call(f32[1,64,4096]{2,1,0:T(8,128)S(1)} %copy-done, s32[128]{0:T(128)S(1)} %bitcast.3, f32[3,16,49]{2,1,0:T(8,128)S(1)} %bitcast.2, s32[16]{0:T(128)S(1)} %copy-done.3, f32[49,128]{1,0:T(8,128)S(1)} %copy-done.6, bf16[4,192,192]{2,1,0:T(8,128)(2,1)S(1)} %copy-done.5, bf16[2,256,1920]{2,1,0:T(8,128)(2,1)S(1)} %copy-done.4), custom_call_target="tpu_custom_call" | custom-call | flops 2000000000 | bytes 4000000 | tf_op jit(solution)/shard_map/pallas_call | solution.py:419
  42.3 0.8 %copy.9 = f32[1,32,4096]{2,1,0:T(8,128)} copy(f32[1,32,4096]{2,1,0:T(8,128)S(1)} %shard_map.73) | data formatting | bytes 1048576
Async XLA Ops:
  0.0 1.2 %copy-start = (f32[1,64,4096]{2,1,0:T(8,128)S(1)}, f32[1,64,4096]{2,1,0:T(8,128)}, u32[]{:S(2)}) copy-start(f32[1,64,4096]{2,1,0:T(8,128)} %image_hbm.1) | copy-start | bytes 3145732
  1.2 0.7 %copy-start.1 = (f32[16,49,3]{1,0,2:T(8,128)S(1)}, f32[16,49,3]{1,0,2:T(8,128)}, u32[]{:S(2)}) copy-start(f32[16,49,3]{1,0,2:T(8,128)} %param.9) | copy-start | bytes 28228
  2.0 0.7 %copy-start.2 = (s32[1,1,128]{2,1,0:T(1,128)S(1)}, s32[1,1,128]{2,1,0:T(1,128)}, u32[]{:S(2)}) copy-start(s32[1,1,128]{2,1,0:T(1,128)} %param.8) | copy-start | bytes 1540
  2.6 0.7 %copy-start.3 = (s32[16]{0:T(128)S(1)}, s32[16]{0:T(128)}, u32[]{:S(2)}) copy-start(s32[16]{0:T(128)} %order_hbm.1) | copy-start | bytes 196
  3.3 1.5 %copy-start.4 = (bf16[2,256,1920]{2,1,0:T(8,128)(2,1)S(1)}, bf16[2,256,1920]{2,1,0:T(8,128)(2,1)}, u32[]{:S(2)}) copy-start(bf16[2,256,1920]{2,1,0:T(8,128)(2,1)} %constant.8.clone.horiz_hbm) | copy-start | bytes 5898244
  4.8 1.0 %copy-start.5 = (bf16[4,192,192]{2,1,0:T(8,128)(2,1)S(1)}, bf16[4,192,192]{2,1,0:T(8,128)(2,1)}, u32[]{:S(2)}) copy-start(bf16[4,192,192]{2,1,0:T(8,128)(2,1)} %constant.7.clone.vert_hbm) | copy-start | bytes 884740
  5.8 0.7 %copy-start.6 = (f32[49,128]{1,0:T(8,128)S(1)}, f32[49,128]{1,0:T(8,128)}, u32[]{:S(2)}) copy-start(f32[49,128]{1,0:T(8,128)} %constant.6.clone.place_hbm) | copy-start | bytes 75268

commit v3 on v2

--- a/solution.py
+++ b/solution.py
@@ -453,7 +453,7 @@
             dma((4, 16)),
         ],
         compiler_params=pltpu.CompilerParams(
-            collective_id=0, has_side_effects=True, vmem_limit_bytes=40 * 1024 * 1024
+            collective_id=0, has_side_effects=True, vmem_limit_bytes=64 * 1024 * 1024 - 4096
         ),
         cost_estimate=pl.CostEstimate(flops=2 * 10**9, bytes_accessed=4 * 10**6, transcendentals=0),
     )(

time: 43.5 us -> 38.5 us (0.89)
  local copies, waits for them, and re-layouts: 7.35 us -> 1.87 us
  Pallas kernels: 35.7 us -> 36.4 us
    unnamed x15 -> x1, local copies, waits for them, and re-layouts: 7.35 us -> 1.87 us
    pallas_call x1, Pallas kernels: 35.7 us -> 36.4 us  [strip(): pl.pallas_call(strip_kernel, out_shape=jax.ShapeDtypeStruct((1, 32, 4096)...]
where the time goes in v3:
time: 38.5 us; the launch traced here: 38.3 us
  Pallas kernels  36.4 us (95%)
  local copies, waits for them, and re-layouts  1.87 us (5%)
    pallas_call x1, Pallas kernels, strip(): pl.pallas_call(strip_kernel, out_shape=jax.ShapeDtypeStruct((1, 32, 4096)...  36.4 us
    unnamed x1, local copies, waits for them, and re-layouts  1.87 us

profile of v3, /device:TPU:0, one launch (start us, length us, event | category | flops | bytes accessed | tf_op | source)
XLA Modules:
  0.0 38.3 jit_solution(2181252256192330646)
XLA Ops:
  0.0 36.4 %shard_map.73 = f32[1,32,4096]{2,1,0:T(8,128)} custom-call(f32[1,64,4096]{2,1,0:T(8,128)} %image_hbm.1, s32[128]{0:T(128)} %bitcast.3, f32[3,16,49]{2,1,0:T(8,128)} %bitcast.2, s32[16]{0:T(128)} %order_hbm.1, f32[49,128]{1,0:T(8,128)} %constant.6.clone.place_hbm, bf16[4,192,192]{2,1,0:T(8,128)(2,1)} %constant.7.clone.vert_hbm, ...), custom_call_target="tpu_custom_call" | custom-call | flops 2000000000 | bytes 4000000 | tf_op jit(solution)/shard_map/pallas_call | solution.py:419
  36.4 1.9 %copy.9 = f32[1,32,4096]{2,1,0:T(8,128)} copy(f32[1,32,4096]{2,1,0:T(8,128)} %shard_map.73) | data formatting | bytes 1048576

commit v4 on v3

--- a/solution.py
+++ b/solution.py
@@ -15,6 +15,7 @@
 KERNELS = 49
 POLY = 3
 LANES = 128
+PIECE = 16
 
 
 gauss_widths = (1.5, 3.0, 6.0)
@@ -170,8 +171,8 @@
             for r in range(rows_out):
                 start = r + MARGIN - HALF
                 vert[g, r, j, start : start + taps.shape[0]] = taps
-    vert = vert.reshape(len(groups), rows_out // 8, 64, padded_rows).swapaxes(0, 1)
-    vert = vert.reshape(rows_out // 8, len(groups) * 64, padded_rows)
+    vert = vert.reshape(len(groups), rows_out // PIECE, 8 * PIECE, padded_rows).swapaxes(0, 1)
+    vert = vert.reshape(rows_out // PIECE, len(groups) * 8 * PIECE, padded_rows)
     high, low = split_constant(vert)
     vert_stack = np.concatenate([high, high, low], axis=2)
     flat = [taps for filters in groups for taps in filters]
@@ -206,8 +207,8 @@
 
 
 def strip_kernel(
-    image_hbm, words_hbm, coef_hbm, order_hbm, place_hbm, vert_hbm, horiz_hbm, out,
-    image, words, coef, order, place, sums, got_core, got_y, got_z, ext, valid, vert, horiz, conv, mix, models, got,
+    image_hbm, words_hbm, coef_hbm, order_hbm, place_hbm, vert_hbm, horiz_hbm, out, valid,
+    image, words, coef, order, place, sums, got_core, got_y, got_z, ext, vert, horiz, conv, mix, models, got,
     load_sem, const_sem, send_core, recv_core, send_y, recv_y, send_z, recv_z, send_halo, recv_halo, send_model, recv_model,
 ):
     count = 16
@@ -252,7 +253,7 @@
                 jnp.where(lane < 96, words[4 * t + 2], words[4 * t + 3]),
             )
             bits = (jnp.right_shift(word, place_bit) & 1).astype(jnp.float32)
-            valid[:, t * LANES : (t + 1) * LANES] = bits
+            valid[:, t * LANES : (t + 1) * LANES] = bits[0:1]
             spot = sums.at[q % 2, (q // 2) % 2, q // 4]
             for s in range(0, 64, 8):
                 spot[s : s + 8, half * LANES : (half + 1) * LANES] = (
@@ -347,17 +348,17 @@
         made = dot32(vert[blk], stacked)
         base = 0
         for g, degree in enumerate(gauss_degrees):
-            rows = made[g * 64 : (g + 1) * 64]
+            rows = made[g * 8 * PIECE : (g + 1) * 8 * PIECE]
             high, low = split(jnp.concatenate([rows[:, :slab], rows[:, slab:]], axis=0))
             outs = slice(base * LANES, (base + degree + 1) * LANES)
             both = dot32(jnp.concatenate([high, low], axis=0), horiz[0, :, outs])
-            conv[:, outs] = both[:LANES] + both[LANES:] + dot32(high, horiz[1, :, outs])
+            conv[:, outs] = both[: 16 * PIECE] + both[16 * PIECE :] + dot32(high, horiz[1, :, outs])
             base += degree + 1
-        for i in range(8):
-            r = blk * 8 + i
+        for i in range(PIECE):
+            r = blk * PIECE + i
             sides = []
             for w in range(2):
-                line = slice(w * 64 + i * 8, w * 64 + i * 8 + 8)
+                line = slice((w * PIECE + i) * 8, (w * PIECE + i + 1) * 8)
                 pieces = [conv[line, h * LANES : (h + 1) * LANES] for h in range(pairs)]
                 pieces.append(jnp.zeros((8, LANES), jnp.float32))
                 sides.append(jnp.concatenate(pieces, axis=0))
@@ -366,30 +367,26 @@
             made = made[: POLY * count] + made[POLY * count :]
             down = (2.0 * lax.convert_element_type(r, jnp.float32) + 1.0) / rows_out - 1.0
             models[:, r, :] = made[:count] + across * made[count : 2 * count] + down * made[2 * count :]
-        start = pl.multiple_of(blk * 8, 8)
+        start = pl.multiple_of(blk * PIECE, PIECE)
         for d in ORDER:
             peer = lax.rem(me + d, count)
             remote(
-                models.at[peer, pl.ds(start, 8)], got.at[me, pl.ds(start, 8)],
+                models.at[peer, pl.ds(start, PIECE)], got.at[me, pl.ds(start, PIECE)],
                 send_model.at[blk, peer], recv_model.at[blk, me], peer,
             ).start()
         return carry
 
-    lax.fori_loop(0, rows_out // 8, model_rows, 0)
+    lax.fori_loop(0, rows_out // PIECE, model_rows, 0)
 
     def finish(q, source):
         start = pl.multiple_of(q * slab, slab)
-        seen = valid[:, pl.ds(start, slab)]
-        for s in range(0, rows_out, 8):
-            out[0, s : s + 8, pl.ds(start, slab)] = seen * (
-                image[0, MARGIN + s : MARGIN + s + 8, pl.ds(start, slab)] - source[q, s : s + 8, :]
-            )
+        out[0, :, pl.ds(start, slab)] = source[q]
 
     finish(me, models)
     for d in ORDER:
         q = lax.rem(me + count - d, count)
-        for blk in range(rows_out // 8):
-            rows = pl.ds(blk * 8, 8)
+        for blk in range(rows_out // PIECE):
+            rows = pl.ds(blk * PIECE, PIECE)
             remote(
                 models.at[q, rows], got.at[q, rows], send_model.at[blk, q], recv_model.at[blk, q], q
             ).wait_recv()
@@ -399,8 +396,8 @@
         copy.wait_send()
     for d in ORDER:
         peer = lax.rem(me + d, count)
-        for blk in range(rows_out // 8):
-            rows = pl.ds(blk * 8, 8)
+        for blk in range(rows_out // PIECE):
+            rows = pl.ds(blk * PIECE, PIECE)
             remote(
                 models.at[peer, rows], got.at[me, rows], send_model.at[blk, peer], recv_model.at[blk, me], peer
             ).wait_send()
@@ -416,11 +413,11 @@
     f32 = jnp.float32
     bf16 = jnp.bfloat16
     dma = pltpu.SemaphoreType.DMA
-    return pl.pallas_call(
+    model, seen = pl.pallas_call(
         strip_kernel,
-        out_shape=jax.ShapeDtypeStruct((1, 32, 4096), f32),
+        out_shape=[jax.ShapeDtypeStruct((1, 32, 4096), f32), jax.ShapeDtypeStruct((1, 4096), f32)],
         in_specs=[hbm] * 7,
-        out_specs=vmem,
+        out_specs=[vmem, vmem],
         scratch_shapes=[
             pltpu.VMEM((1, 64, 4096), f32),
             pltpu.SMEM((128,), jnp.int32),
@@ -432,10 +429,9 @@
             pltpu.VMEM((4, 64, 256), f32),
             pltpu.VMEM((4, 64, 256), f32),
             pltpu.VMEM((64, 512), f32),
-            pltpu.VMEM((8, 4096), f32),
             pltpu.VMEM(vert.shape, bf16),
             pltpu.VMEM(horiz.shape, bf16),
-            pltpu.VMEM((128, 15 * LANES), f32),
+            pltpu.VMEM((16 * PIECE, 15 * LANES), f32),
             pltpu.VMEM((96, 256), bf16),
             pltpu.VMEM((16, 32, 256), f32),
             pltpu.VMEM((16, 32, 256), f32),
@@ -449,8 +445,8 @@
             dma((4,)),
             dma((2,)),
             dma((2,)),
-            dma((4, 16)),
-            dma((4, 16)),
+            dma((32 // PIECE, 16)),
+            dma((32 // PIECE, 16)),
         ],
         compiler_params=pltpu.CompilerParams(
             collective_id=0, has_side_effects=True, vmem_limit_bytes=64 * 1024 * 1024 - 4096
@@ -465,6 +461,7 @@
         jnp.asarray(vert),
         jnp.asarray(horiz),
     )
+    return seen[None] * (epoch_images[:, MARGIN : MARGIN + 32] - model)
 
 
 def solution(mesh):

time: 38.5 us -> 38.3 us (level)
  other arithmetic: 0 us -> 2.06 us
  local copies, waits for them, and re-layouts: 1.87 us -> 0 us
    mul x0 -> x1, other arithmetic: none -> 2.06 us  [strip(): return seen[None] * (epoch_images[:, MARGIN:MARGIN + 32] - model)]
    unnamed x1 -> x0, local copies, waits for them, and re-layouts: 1.87 us -> none
where the time goes in v4:
time: 38.3 us; the launch traced here: 38.2 us
  Pallas kernels  36.1 us (94%)
  other arithmetic  2.06 us (5%)
    pallas_call x1, Pallas kernels, strip(): pl.pallas_call(strip_kernel, out_shape=[jax.ShapeDtypeStruct((1, 32, 4096...  36.1 us
    mul x1, other arithmetic, strip(): return seen[None] * (epoch_images[:, MARGIN:MARGIN + 32] - model)  2.06 us

profile of v4, /device:TPU:0, one launch (start us, length us, event | category | flops | bytes accessed | tf_op | source)
XLA Modules:
  0.0 38.2 jit_solution(15753894628006899068)
XLA Ops:
  0.0 36.1 %shard_map.73 = (f32[1,32,4096]{2,1,0:T(8,128)}, f32[1,4096]{1,0:T(1,128)}) custom-call(f32[1,64,4096]{2,1,0:T(8,128)} %image_hbm.1, s32[128]{0:T(128)} %bitcast.5, f32[3,16,49]{2,1,0:T(8,128)} %bitcast.4, s32[16]{0:T(128)} %order_hbm.1, f32[49,128]{1,0:T(8,128)} %constant.6.clone.place_hbm, bf16[2,384,192]{2,1,0:T(8,128)(2,1)} %constant.7.clone.vert_hbm, ...), custom_call_target="tpu_custom_call" | custom-call | flops 2000000000 | bytes 4000000 | tf_op jit(solution)/shard_map/pallas_call | solution.py:416
  36.1 2.1 %subtract_multiply_fusion = f32[1,32,4096]{2,1,0:T(8,128)} fusion(f32[1,32,4096]{2,1,0:T(8,128)} %get-tuple-element.8, f32[1,64,4096]{2,1,0:T(8,128)} %image_hbm.1, f32[4096]{0:T(1024)} %bitcast.3), kind=kLoop, calls=%fused_computation | loop fusion | flops 262144 | bytes 1589248 | tf_op jit(solution)/shard_map/mul | solution.py:464

commit v5 on v4

--- a/solution.py
+++ b/solution.py
@@ -449,7 +449,7 @@
             dma((32 // PIECE, 16)),
         ],
         compiler_params=pltpu.CompilerParams(
-            collective_id=0, has_side_effects=True, vmem_limit_bytes=64 * 1024 * 1024 - 4096
+            collective_id=0, has_side_effects=True, vmem_limit_bytes=64 * 1024 * 1024 - 589824
         ),
         cost_estimate=pl.CostEstimate(flops=2 * 10**9, bytes_accessed=4 * 10**6, transcendentals=0),
     )(

time: 38.3 us -> 38.3 us (level)
  no operation moved by 1% of the time
where the time goes in v5:
time: 38.3 us; the launch traced here: 38.2 us
  Pallas kernels  36.1 us (94%)
  other arithmetic  2.06 us (5%)
    pallas_call x1, Pallas kernels, strip(): pl.pallas_call(strip_kernel, out_shape=[jax.ShapeDtypeStruct((1, 32, 4096...  36.1 us
    mul x1, other arithmetic, strip(): return seen[None] * (epoch_images[:, MARGIN:MARGIN + 32] - model)  2.06 us

profile of v5, /device:TPU:0, one launch (start us, length us, event | category | flops | bytes accessed | tf_op | source)
XLA Modules:
  0.0 38.2 jit_solution(15753894628006899068)
XLA Ops:
  0.0 36.1 %shard_map.73 = (f32[1,32,4096]{2,1,0:T(8,128)}, f32[1,4096]{1,0:T(1,128)}) custom-call(f32[1,64,4096]{2,1,0:T(8,128)} %image_hbm.1, s32[128]{0:T(128)} %bitcast.5, f32[3,16,49]{2,1,0:T(8,128)} %bitcast.4, s32[16]{0:T(128)} %order_hbm.1, f32[49,128]{1,0:T(8,128)} %constant.6.clone.place_hbm, bf16[2,384,192]{2,1,0:T(8,128)(2,1)} %constant.7.clone.vert_hbm, ...), custom_call_target="tpu_custom_call" | custom-call | flops 2000000000 | bytes 4000000 | tf_op jit(solution)/shard_map/pallas_call | solution.py:416
  36.1 2.1 %subtract_multiply_fusion = f32[1,32,4096]{2,1,0:T(8,128)} fusion(f32[1,32,4096]{2,1,0:T(8,128)} %get-tuple-element.8, f32[1,64,4096]{2,1,0:T(8,128)} %image_hbm.1, f32[4096]{0:T(1024)} %bitcast.3), kind=kLoop, calls=%fused_computation | loop fusion | flops 262144 | bytes 1589248 | tf_op jit(solution)/shard_map/mul | solution.py:464

commit v6 on v4

--- a/solution.py
+++ b/solution.py
@@ -263,27 +263,31 @@
     pl.semaphore_wait(barrier, count - 1)
 
     core_copies = []
-    for h, yy in enumerate((1 - y, y)):
+    ring = [lax.rem(z + d, zs) for d in (2, 1, 3, 0)]
+    other = me + 1 - 2 * k
+    for h, zz in enumerate(ring):
         copy = remote(
-            sums.at[1 - k, yy], got_core.at[yy], send_core.at[h], recv_core.at[h], me + 1 - 2 * k
+            sums.at[1 - k, 1 - y, zz], got_core.at[1 - y, zz], send_core.at[h], recv_core.at[h], other
         )
         copy.start()
         core_copies.append(copy)
+    copy = remote(sums.at[1 - k, y], got_core.at[y], send_core.at[zs], recv_core.at[zs], other)
+    copy.start()
+    core_copies.append(copy)
     constants = []
     sources = (order_hbm, coef_hbm, place_hbm, vert_hbm, horiz_hbm)
     for c, (src, dst) in enumerate(zip(sources, (order, coef, place, vert, horiz))):
         load = pltpu.make_async_copy(src, dst, const_sem.at[c])
         load.start()
         constants.append(load)
-    core_copies[0].wait_recv()
-    ring = [lax.rem(z + d, zs) for d in (2, 1, 3, 0)]
     y_copies = []
-    for zz in ring:
+    for zz, arrived in zip(ring, core_copies):
+        arrived.wait_recv()
         sums[k, 1 - y, zz] = sums[k, 1 - y, zz] + got_core[1 - y, zz]
         copy = remote(sums.at[k, 1 - y, zz], got_y.at[zz], send_y.at[zz], recv_y.at[zz], me + 2 - 4 * y)
         copy.start()
         y_copies.append(copy)
-    core_copies[1].wait_recv()
+    core_copies[zs].wait_recv()
     for zz in ring:
         sums[k, y, zz] = sums[k, y, zz] + got_core[y, zz]
 
@@ -437,8 +441,8 @@
             pltpu.VMEM((16, 32, 256), f32),
             dma((5,)),
             dma((5,)),
-            dma((2,)),
-            dma((2,)),
+            dma((5,)),
+            dma((5,)),
             dma((4,)),
             dma((4,)),
             dma((4,)),

time: 38.3 us -> 38.1 us (level)
  no operation moved by 1% of the time
where the time goes in v6:
time: 38.1 us; the launch traced here: 37.9 us
  Pallas kernels  35.9 us (94%)
  other arithmetic  2.06 us (5%)
    pallas_call x1, Pallas kernels, strip(): pl.pallas_call(strip_kernel, out_shape=[jax.ShapeDtypeStruct((1, 32, 4096...  35.9 us
    mul x1, other arithmetic, strip(): return seen[None] * (epoch_images[:, MARGIN:MARGIN + 32] - model)  2.06 us

profile of v6, /device:TPU:0, one launch (start us, length us, event | category | flops | bytes accessed | tf_op | source)
XLA Modules:
  0.0 37.9 jit_solution(16903848954878357795)
XLA Ops:
  0.0 35.9 %shard_map.73 = (f32[1,32,4096]{2,1,0:T(8,128)}, f32[1,4096]{1,0:T(1,128)}) custom-call(f32[1,64,4096]{2,1,0:T(8,128)} %image_hbm.1, s32[128]{0:T(128)} %bitcast.5, f32[3,16,49]{2,1,0:T(8,128)} %bitcast.4, s32[16]{0:T(128)} %order_hbm.1, f32[49,128]{1,0:T(8,128)} %constant.6.clone.place_hbm, bf16[2,384,192]{2,1,0:T(8,128)(2,1)} %constant.7.clone.vert_hbm, ...), custom_call_target="tpu_custom_call" | custom-call | flops 2000000000 | bytes 4000000 | tf_op jit(solution)/shard_map/pallas_call | solution.py:420
  35.9 2.1 %subtract_multiply_fusion = f32[1,32,4096]{2,1,0:T(8,128)} fusion(f32[1,32,4096]{2,1,0:T(8,128)} %get-tuple-element.8, f32[1,64,4096]{2,1,0:T(8,128)} %image_hbm.1, f32[4096]{0:T(1024)} %bitcast.3), kind=kLoop, calls=%fused_computation | loop fusion | flops 262144 | bytes 1589248 | tf_op jit(solution)/shard_map/mul | solution.py:468
